TPU v7x, 32 devices: a whole 2x2x4 slice. The times are simulated.
32 devices in a mesh: dp: 4 (over x, core), clique: 8 (over z, y).
Axes of the slice: x: 2, y: 2, z: 4, core: 2. Of those that a mesh axis runs over, the one named last changes fastest.
Arguments:
- table_rows: int32 [9, 262144], P(None, 'dp'), may hold values from 0 to 255
- attribute_order: int32 [9], replicated, may hold values from 0 to 8, each once
- log_potential: float32 [8, 256, 256], P('clique'), may hold values from -4 to 18
- measure_noise: float32 [8, 256, 256], P('clique'), may hold values from -24 to 24
Outputs:
- updated_potentials: float32 [8, 256, 256], P('clique')
- beliefs: float32 [8, 256, 256], P('clique')
Inputs may be any that keep to these rules, and one draw needn't show every extreme that they name: `attribute_order`: each of the 9 attributes appears once.
All inputs are finite; a program needn't handle non-finite values.
Results may differ from a plain program's by a relative error of at most 0.0003.
Values sent between devices are 32-bit elements; how exact they have to be, the bound alone decides.
A program may use at most 128 MiB of HBM per device.

v0:
```python
import functools
import math

import jax
import jax.numpy as jnp
from jax import lax
from jax.experimental import pallas as pl
from jax.experimental.pallas import tpu as pltpu
from jax.sharding import PartitionSpec as P

step_size = 0.25
PIECES = 4
BLOCK = 4096
QUARTERS = 4
MEET = 4
VMEM_LIMIT = 60 * 1024 * 1024
MESH = pl.DeviceIdType.MESH
BF16 = jnp.bfloat16
F32 = jnp.float32
ONE = jnp.float8_e4m3fn


def split_high_low(value):
    high = value.astype(BF16)
    return high, (value - high.astype(F32)).astype(BF16)


def message_rows(vector):
    wide = jnp.broadcast_to(vector, (16, vector.shape[1]))
    high = wide.astype(BF16).astype(F32)
    row = lax.broadcasted_iota(jnp.int32, wide.shape, 0)
    return jnp.where(row < 8, high, wide - high).astype(BF16)


def carry(vector, kernel_high, kernel_low, contract):
    rows = message_rows(vector)
    dims = (((1,), (contract,)), ((), ()))
    moved = lax.dot_general(rows, kernel_high[...], dims, preferred_element_type=F32)
    moved += lax.dot_general(rows, kernel_low[...], dims, preferred_element_type=F32)
    return (moved[0:1] + moved[8:9]) / jnp.sum(vector)


def fill_one_hot(tab, attribute, start, levels, slot):
    kinds, deep, lanes = levels.shape
    width = slot.shape[1]
    values = tab[pl.ds(attribute, 1), pl.ds(pl.multiple_of(start, width), width)] - 128
    for tile in range(0, width, lanes):
        wide = jnp.broadcast_to(values[:, tile : tile + lanes], (deep, lanes))
        hit = wide.astype(jnp.int8)[None] == levels
        ones = jnp.where(hit, jnp.ones((), ONE), jnp.zeros((), ONE))
        slot[:, tile : tile + lanes] = ones.reshape(kinds * deep, lanes)


def kernel(
    sizes, scale, order, table, potential_in, noise_in, updated_out, beliefs_out,
    tabs, slots, potential, noise, updated, beliefs, acc, q, q_high, q_low, m_high, m_low,
    vectors, sibling, half, across, total,
    tab_sem, in_sem, out_sem, pair_sem, f_sem, g_sem, send1, recv1, send2, recv2, send3, recv3,
):
    cliques, copies = sizes
    f_in, f_out, g_in, g_out, f_own, g_own = vectors
    domain = acc.shape[0]
    groups = cliques // 2
    columns = tabs[0].shape[1]
    blocks = columns // BLOCK
    chips = copies // 2
    rows = domain // 2 // PIECES
    k = lax.axis_index("clique")
    d = lax.axis_index("dp")
    chip, core = d // 2, lax.rem(d, 2)
    twin = chip * 2 + 1 - core
    group, odd = k // 2, lax.rem(k, 2)
    partner = group * 2 + 1 - odd

    get_potential = pltpu.make_async_copy(
        potential_in.at[0], potential.at[odd], in_sem.at[0]
    )
    get_potential.start()
    loads = []
    for quarter, tab in enumerate(tabs):
        where = pl.ds(quarter * columns, columns)
        load = pltpu.make_async_copy(table.at[:, where], tab, tab_sem.at[quarter])
        load.start()
        loads.append(load)
    get_noise = pltpu.make_async_copy(noise_in.at[0], noise, in_sem.at[1])
    get_noise.start()

    barrier = pltpu.get_barrier_semaphore()

    def greet(device):
        pl.semaphore_signal(barrier, inc=1, device_id=device, device_id_type=MESH)

    greet({"dp": twin})
    for step in range(1, chips):
        greet({"dp": lax.rem(chip + step, chips) * 2 + core})

    greet({"clique": partner})

    @pl.when(group > 0)
    def _():
        greet({"clique": k - 2})

    @pl.when(group < groups - 1)
    def _():
        greet({"clique": k + 2})

    acc[...] = jnp.zeros_like(acc)
    slots[1][0][...] = jnp.zeros_like(slots[1][0])
    slots[1][1][...] = jnp.zeros_like(slots[1][1])

    @pl.when(group == 0)
    def _():
        f_in[...] = jnp.ones_like(f_in)

    @pl.when(group == groups - 1)
    def _():
        g_in[...] = jnp.ones_like(g_in)

    at_end = jnp.logical_or(group == 0, group == groups - 1)

    @pl.when(at_end)
    def _():
        pl.semaphore_wait(barrier, chips + 2)

    @pl.when(jnp.logical_not(at_end))
    def _():
        pl.semaphore_wait(barrier, chips + 3)

    pair_copy = pltpu.make_async_remote_copy(
        potential_in.at[0], potential.at[odd], pair_sem.at[0], pair_sem.at[1],
        {"clique": partner}, MESH,
    )
    pair_copy.start()
    f_copy = pltpu.make_async_remote_copy(
        f_out, f_in, f_sem.at[0], f_sem.at[1], {"clique": lax.rem(k + 2, cliques)}, MESH
    )
    g_copy = pltpu.make_async_remote_copy(
        g_out, g_in, g_sem.at[0], g_sem.at[1],
        {"clique": lax.rem(k + cliques - 2, cliques)}, MESH,
    )

    def prepare(which):
        q[which] = jnp.exp(potential[which])
        q_high[which], q_low[which] = split_high_low(q[which])

    get_potential.wait()
    prepare(odd)

    def pair_product():
        pair_copy.wait_recv()
        prepare(1 - odd)
        product = jnp.dot(q_high[0], q_high[1], preferred_element_type=F32)
        product += jnp.dot(q_high[0], q_low[1], preferred_element_type=F32)
        product += jnp.dot(q_low[0], q_high[1], preferred_element_type=F32)
        m_high[...], m_low[...] = split_high_low(product)

    def stage(number):
        @pl.when(group == number)
        def _():
            if number > 0:
                f_copy.wait_recv()
            if number < groups - 1:
                f_out[...] = carry(f_in[...], m_high, m_low, 0)
                f_copy.start()

        @pl.when(group == groups - 1 - number)
        def _():
            if number > 0:
                g_copy.wait_recv()
            if number < groups - 1:
                g_out[...] = carry(g_in[...], m_high, m_low, 1)
                g_copy.start()

    left, right = order[k], order[k + 1]
    pairs = blocks // 2
    meet = min(MEET, QUARTERS * pairs - 1)
    shape = (domain // 32, 32, 128)
    level = lax.broadcasted_iota(jnp.int32, shape, 0) * 32
    level += lax.broadcasted_iota(jnp.int32, shape, 1)
    levels = (level - 128).astype(jnp.int8)

    def multiply(slot):
        acc[...] += lax.dot_general(
            slot[0][...], slot[1][...], (((1,), (1,)), ((), ())),
            preferred_element_type=F32,
        )

    for quarter, tab in enumerate(tabs):
        loads[quarter].wait()

        @pl.loop(0, pairs)
        def _(pair, tab=tab, quarter=quarter):
            for turn in range(2):
                multiply(slots[1 - turn])
                start = (pair * 2 + turn) * BLOCK
                fill_one_hot(tab, left, start, levels, slots[turn][0])
                fill_one_hot(tab, right, start, levels, slots[turn][1])

            @pl.when(quarter * pairs + pair == meet)
            def _():
                pair_product()
                stage(0)

            if groups > 2:

                @pl.when(quarter * pairs + pair == min(meet + 2, QUARTERS * pairs - 1))
                def _():
                    stage(1)

    multiply(slots[1])
    mine, theirs = core * (domain // 2), (1 - core) * (domain // 2)

    def part(base, piece):
        return pl.ds(pl.multiple_of(base + piece * rows, rows), rows)

    first_trip, second_trip, third_trip = [], [], []
    for piece in range(PIECES):
        copy = pltpu.make_async_remote_copy(
            acc.at[part(theirs, piece)], sibling.at[piece],
            send1.at[piece], recv1.at[piece], {"dp": twin}, MESH,
        )
        copy.start()
        first_trip.append(copy)
    for number in range(2, groups - 1):
        stage(number)
    for piece in range(PIECES):
        first_trip[piece].wait_recv()
        half[piece] = acc[part(mine, piece), :] + sibling[piece]
        for step in range(1, chips):
            copy = pltpu.make_async_remote_copy(
                half.at[piece], across.at[step - 1, piece],
                send2.at[step - 1, piece], recv2.at[step - 1, piece],
                {"dp": lax.rem(chip + step, chips) * 2 + core}, MESH,
            )
            copy.start()
            second_trip.append(copy)

    if groups > 1:
        stage(groups - 1)

    @pl.when(odd == 1)
    def _():
        f_own[...] = carry(f_in[...], q_high.at[0], q_low.at[0], 0)
        g_own[...] = g_in[...]

    @pl.when(odd == 0)
    def _():
        f_own[...] = f_in[...]
        g_own[...] = carry(g_in[...], q_high.at[1], q_low.at[1], 1)

    f, g = f_own[...], g_own[...]
    column = jnp.transpose(jnp.broadcast_to(f / jnp.sum(f), (8, domain)))[:, 0:1]
    joint = column * q[odd] * (g / jnp.sum(g))
    beliefs[...] = joint * (float(domain * domain) / jnp.sum(joint))

    put_beliefs = pltpu.make_async_copy(beliefs, beliefs_out, out_sem.at[0])
    put_beliefs.start()

    for piece in range(PIECES):
        summed = half[piece]
        for step in range(1, chips):
            second_trip[piece * (chips - 1) + step - 1].wait_recv()
            summed = summed + across[step - 1, piece]
        total[part(mine, piece), :] = summed
        copy = pltpu.make_async_remote_copy(
            total.at[part(mine, piece)], total.at[part(mine, piece)],
            send3.at[piece], recv3.at[piece], {"dp": twin}, MESH,
        )
        copy.start()
        third_trip.append(copy)

    get_noise.wait()

    def finish(where):
        measured = (total[where, :] + noise[where, :]) * scale
        updated[where, :] = potential[odd, where, :] - step_size * (beliefs[where, :] - measured)

    halves = []
    for number, base in enumerate((mine, theirs)):
        for piece in range(PIECES):
            if number == 1:
                third_trip[piece].wait_recv()
            finish(part(base, piece))
        where = pl.ds(pl.multiple_of(base, domain // 2), domain // 2)
        put = pltpu.make_async_copy(
            updated.at[where], updated_out.at[where], out_sem.at[1 + number]
        )
        put.start()
        halves.append(put)

    for copy in first_trip + second_trip + third_trip:
        copy.wait_send()

    pair_copy.wait_send()
    for copy in [put_beliefs] + halves:
        copy.wait()

    @pl.when(group < groups - 1)
    def _():
        f_copy.wait_send()

    @pl.when(group > 0)
    def _():
        g_copy.wait_send()


def hand_on(updated, beliefs, updated_out, beliefs_out, held, get_sem, put_sem):
    rows = updated.shape[0] // 2
    parts = []
    for number, (source, target) in enumerate(((updated, updated_out), (beliefs, beliefs_out))):
        for half in range(2):
            where, slot = pl.ds(half * rows, rows), held.at[number, half]
            get = pltpu.make_async_copy(source.at[where], slot, get_sem.at[number, half])
            put = pltpu.make_async_copy(slot, target.at[where], put_sem.at[number, half])
            get.start()
            parts.append((get, put))
    for get, put in parts:
        get.wait()
        put.start()
    for get, put in parts:
        put.wait()


def per_device(table_rows, attribute_order, log_potential, measure_noise):
    cliques, copies = lax.axis_size("clique"), lax.axis_size("dp")
    domain = log_potential.shape[1]
    attributes, columns = table_rows.shape
    scale = domain * domain / (columns * copies)
    rows = domain // 2 // PIECES
    chips = copies // 2
    table = jax.ShapeDtypeStruct((domain, domain), F32)
    hbm = pl.BlockSpec(memory_space=pl.ANY)
    dma = pltpu.SemaphoreType.DMA
    updated, beliefs = pl.pallas_call(
        functools.partial(kernel, (cliques, copies), scale),
        out_shape=(table, table),
        in_specs=[
            pl.BlockSpec(memory_space=pltpu.SMEM),
            hbm,
            hbm,
            hbm,
        ],
        out_specs=(hbm, hbm),
        scratch_shapes=[
            [pltpu.VMEM((attributes, columns // QUARTERS), jnp.int32)] * QUARTERS,
            [[pltpu.VMEM((domain, BLOCK), ONE)] * 2] * 2,
            pltpu.VMEM((2, domain, domain), F32),
            pltpu.VMEM((domain, domain), F32),
            pltpu.VMEM((domain, domain), F32),
            pltpu.VMEM((domain, domain), F32),
            pltpu.VMEM((domain, domain), F32),
            pltpu.VMEM((2, domain, domain), F32),
            pltpu.VMEM((2, domain, domain), BF16),
            pltpu.VMEM((2, domain, domain), BF16),
            pltpu.VMEM((domain, domain), BF16),
            pltpu.VMEM((domain, domain), BF16),
            [pltpu.VMEM((1, domain), F32)] * 6,
            pltpu.VMEM((PIECES, rows, domain), F32),
            pltpu.VMEM((PIECES, rows, domain), F32),
            pltpu.VMEM((chips - 1, PIECES, rows, domain), F32),
            pltpu.VMEM((domain, domain), F32),
            dma((QUARTERS,)),
            dma((2,)),
            dma((3,)),
            dma((2,)),
            dma((2,)),
            dma((2,)),
            dma((PIECES,)),
            dma((PIECES,)),
            dma((chips - 1, PIECES)),
            dma((chips - 1, PIECES)),
            dma((PIECES,)),
            dma((PIECES,)),
        ],
        compiler_params=pltpu.CompilerParams(
            collective_id=0, has_side_effects=True, vmem_limit_bytes=VMEM_LIMIT
        ),
    )(attribute_order, table_rows, log_potential, measure_noise)
    updated, beliefs = pl.pallas_call(
        hand_on,
        out_shape=(table, table),
        in_specs=[hbm, hbm],
        out_specs=(hbm, hbm),
        scratch_shapes=[
            pltpu.VMEM((2, 2, domain // 2, domain), F32), dma((2, 2)), dma((2, 2)),
        ],
        compiler_params=pltpu.CompilerParams(vmem_limit_bytes=VMEM_LIMIT),
    )(updated, beliefs)
    return updated[None], beliefs[None]


def solution(mesh):
    in_specs = (P(None, "dp"), P(), P("clique", None, None), P("clique", None, None))
    out_specs = (P("clique", None, None), P("clique", None, None))
    return jax.shard_map(
        per_device, mesh=mesh, in_specs=in_specs, out_specs=out_specs, check_vma=False
    )
```

profile of v0, /device:TPU:1, one launch (start us, length us, event | category | flops | bytes accessed | tf_op | source)
XLA Modules:
  0.0 26.8 jit_solution(1288025730891568146)
XLA Ops:
  0.6 24.3 %shard_map.59 = (f32[256,256]{1,0:T(8,128)}, f32[256,256]{1,0:T(8,128)}) custom-call(s32[9]{0:T(128)} %order.1, s32[9,65536]{1,0:T(8,128)} %table.1, f32[1,256,256]{2,1,0:T(8,128)} %potential_in.1, f32[1,256,256]{2,1,0:T(8,128)} %noise_in.1), custom_call_target="tpu_custom_call" | custom-call | tf_op jit(solution)/shard_map/pallas_call | solution.py:334
  25.0 1.8 %shard_map.60 = (f32[256,256]{1,0:T(8,128)}, f32[256,256]{1,0:T(8,128)}) custom-call(f32[256,256]{1,0:T(8,128)} %get-tuple-element.6.updated, f32[256,256]{1,0:T(8,128)} %get-tuple-element.7.beliefs), custom_call_target="tpu_custom_call" | custom-call | tf_op jit(solution)/shard_map/pallas_call | solution.py:379
where the time goes:
time: 27 us; the launch traced here: 26.8 us
  Pallas kernels  26.2 us (97%)
  between operations  0.64 us (2%)
    pallas_call x1, Pallas kernels, per_device(): pl.pallas_call(functools.partial(kernel, (cliques, copies), scale), out_s...  24.3 us
    pallas_call x1, Pallas kernels, per_device(): pl.pallas_call(hand_on, out_shape=(table, table), in_specs=[hbm, hbm], ou...  1.82 us

commit v1 on v0

--- a/solution.py
+++ b/solution.py
@@ -108,23 +108,28 @@
     slots[1][0][...] = jnp.zeros_like(slots[1][0])
     slots[1][1][...] = jnp.zeros_like(slots[1][1])
 
-    @pl.when(group == 0)
+    @pl.when(k == 0)
     def _():
         f_in[...] = jnp.ones_like(f_in)
 
-    @pl.when(group == groups - 1)
+    @pl.when(k == cliques - 1)
     def _():
         g_in[...] = jnp.ones_like(g_in)
 
-    at_end = jnp.logical_or(group == 0, group == groups - 1)
-
-    @pl.when(at_end)
-    def _():
-        pl.semaphore_wait(barrier, chips + 2)
-
-    @pl.when(jnp.logical_not(at_end))
-    def _():
-        pl.semaphore_wait(barrier, chips + 3)
+    second, before_last = k == 1, k == cliques - 2
+
+    @pl.when(jnp.logical_or(second, k == cliques - 3))
+    def _():
+        greet({"clique": k + 1})
+
+    @pl.when(jnp.logical_or(k == 2, before_last))
+    def _():
+        greet({"clique": k - 1})
+
+    inner = jnp.logical_and(group > 0, group < groups - 1)
+    crossing = (k == 1, k == 2, k == cliques - 3, k == cliques - 2)
+    extra = sum(jnp.where(one, 1, 0) for one in crossing)
+    pl.semaphore_wait(barrier, chips + 2 + jnp.where(inner, 1, 0) + extra)
 
     pair_copy = pltpu.make_async_remote_copy(
         potential_in.at[0], potential.at[odd], pair_sem.at[0], pair_sem.at[1],
@@ -132,11 +137,20 @@
     )
     pair_copy.start()
     f_copy = pltpu.make_async_remote_copy(
-        f_out, f_in, f_sem.at[0], f_sem.at[1], {"clique": lax.rem(k + 2, cliques)}, MESH
+        f_out, f_in, f_sem.at[0], f_sem.at[1],
+        {"clique": jnp.where(k == 0, 1, lax.rem(k + 2, cliques))}, MESH,
+    )
+    f_cross = pltpu.make_async_remote_copy(
+        f_out, f_in, f_sem.at[2], f_sem.at[1], {"clique": lax.rem(k + 1, cliques)}, MESH
     )
     g_copy = pltpu.make_async_remote_copy(
         g_out, g_in, g_sem.at[0], g_sem.at[1],
-        {"clique": lax.rem(k + cliques - 2, cliques)}, MESH,
+        {"clique": jnp.where(k == cliques - 1, k - 1, lax.rem(k + cliques - 2, cliques))},
+        MESH,
+    )
+    g_cross = pltpu.make_async_remote_copy(
+        g_out, g_in, g_sem.at[2], g_sem.at[1],
+        {"clique": lax.rem(k + cliques - 1, cliques)}, MESH,
     )
 
     def prepare(which):
@@ -146,27 +160,53 @@
     get_potential.wait()
     prepare(odd)
 
+    @pl.when(k == 0)
+    def _():
+        f_out[...] = carry(f_in[...], q_high.at[0], q_low.at[0], 0)
+        f_copy.start()
+
+    @pl.when(k == cliques - 1)
+    def _():
+        g_out[...] = carry(g_in[...], q_high.at[1], q_low.at[1], 1)
+        g_copy.start()
+
+    def second_messages():
+        @pl.when(second)
+        def _():
+            f_copy.wait_recv()
+            f_out[...] = carry(f_in[...], q_high.at[1], q_low.at[1], 0)
+            f_copy.start()
+            f_cross.start()
+
+        @pl.when(before_last)
+        def _():
+            g_copy.wait_recv()
+            g_out[...] = carry(g_in[...], q_high.at[0], q_low.at[0], 1)
+            g_copy.start()
+            g_cross.start()
+
     def pair_product():
         pair_copy.wait_recv()
         prepare(1 - odd)
-        product = jnp.dot(q_high[0], q_high[1], preferred_element_type=F32)
-        product += jnp.dot(q_high[0], q_low[1], preferred_element_type=F32)
-        product += jnp.dot(q_low[0], q_high[1], preferred_element_type=F32)
-        m_high[...], m_low[...] = split_high_low(product)
+
+        @pl.when(inner)
+        def _():
+            product = jnp.dot(q_high[0], q_high[1], preferred_element_type=F32)
+            product += jnp.dot(q_high[0], q_low[1], preferred_element_type=F32)
+            product += jnp.dot(q_low[0], q_high[1], preferred_element_type=F32)
+            m_high[...], m_low[...] = split_high_low(product)
 
     def stage(number):
         @pl.when(group == number)
         def _():
-            if number > 0:
-                f_copy.wait_recv()
+            f_copy.wait_recv()
             if number < groups - 1:
                 f_out[...] = carry(f_in[...], m_high, m_low, 0)
                 f_copy.start()
 
         @pl.when(group == groups - 1 - number)
         def _():
-            if number > 0:
-                g_copy.wait_recv()
+            g_copy.wait_recv()
             if number < groups - 1:
                 g_out[...] = carry(g_in[...], m_high, m_low, 1)
                 g_copy.start()
@@ -196,16 +236,13 @@
                 fill_one_hot(tab, left, start, levels, slots[turn][0])
                 fill_one_hot(tab, right, start, levels, slots[turn][1])
 
-            @pl.when(quarter * pairs + pair == meet)
+            done = quarter * pairs + pair
+            pl.when(done == 1)(second_messages)
+
+            @pl.when(done == meet)
             def _():
                 pair_product()
-                stage(0)
-
-            if groups > 2:
-
-                @pl.when(quarter * pairs + pair == min(meet + 2, QUARTERS * pairs - 1))
-                def _():
-                    stage(1)
+                stage(1)
 
     multiply(slots[1])
     mine, theirs = core * (domain // 2), (1 - core) * (domain // 2)
@@ -235,17 +272,17 @@
             copy.start()
             second_trip.append(copy)
 
-    if groups > 1:
-        stage(groups - 1)
-
-    @pl.when(odd == 1)
+    stage(groups - 1)
+
+    f_own[...] = f_in[...]
+    g_own[...] = g_in[...]
+
+    @pl.when(jnp.logical_and(odd == 1, k > 1))
     def _():
         f_own[...] = carry(f_in[...], q_high.at[0], q_low.at[0], 0)
-        g_own[...] = g_in[...]
-
-    @pl.when(odd == 0)
-    def _():
-        f_own[...] = f_in[...]
+
+    @pl.when(jnp.logical_and(odd == 0, k < cliques - 2))
+    def _():
         g_own[...] = carry(g_in[...], q_high.at[1], q_low.at[1], 1)
 
     f, g = f_own[...], g_own[...]
@@ -302,6 +339,14 @@
     @pl.when(group > 0)
     def _():
         g_copy.wait_send()
+
+    @pl.when(second)
+    def _():
+        f_cross.wait_send()
+
+    @pl.when(before_last)
+    def _():
+        g_cross.wait_send()
 
 
 def hand_on(updated, beliefs, updated_out, beliefs_out, held, get_sem, put_sem):
@@ -363,8 +408,8 @@
             dma((2,)),
             dma((3,)),
             dma((2,)),
-            dma((2,)),
-            dma((2,)),
+            dma((3,)),
+            dma((3,)),
             dma((PIECES,)),
             dma((PIECES,)),
             dma((chips - 1, PIECES)),

time: 27 us -> 26.7 us (0.989)
  Pallas kernels: 26.2 us -> 25.9 us
where the time goes in v1:
time: 26.7 us; the launch traced here: 26.5 us
  Pallas kernels  25.9 us (97%)
  between operations  0.64 us (2%)
    pallas_call x1, Pallas kernels, per_device(): pl.pallas_call(functools.partial(kernel, (cliques, copies), scale), out_s...  24.1 us
    pallas_call x1, Pallas kernels, per_device(): pl.pallas_call(hand_on, out_shape=(table, table), in_specs=[hbm, hbm], ou...  1.82 us

profile of v1, /device:TPU:1, one launch (start us, length us, event | category | flops | bytes accessed | tf_op | source)
XLA Modules:
  0.0 26.5 jit_solution(18125905198603627215)
XLA Ops:
  0.6 24.1 %shard_map.59 = (f32[256,256]{1,0:T(8,128)}, f32[256,256]{1,0:T(8,128)}) custom-call(s32[9]{0:T(128)} %order.1, s32[9,65536]{1,0:T(8,128)} %table.1, f32[1,256,256]{2,1,0:T(8,128)} %potential_in.1, f32[1,256,256]{2,1,0:T(8,128)} %noise_in.1), custom_call_target="tpu_custom_call" | custom-call | tf_op jit(solution)/shard_map/pallas_call | solution.py:379
  24.7 1.8 %shard_map.60 = (f32[256,256]{1,0:T(8,128)}, f32[256,256]{1,0:T(8,128)}) custom-call(f32[256,256]{1,0:T(8,128)} %get-tuple-element.6.updated, f32[256,256]{1,0:T(8,128)} %get-tuple-element.7.beliefs), custom_call_target="tpu_custom_call" | custom-call | tf_op jit(solution)/shard_map/pallas_call | solution.py:424

commit v2 on v1

--- a/solution.py
+++ b/solution.py
@@ -12,7 +12,8 @@
 PIECES = 4
 BLOCK = 4096
 QUARTERS = 4
-MEET = 4
+RELAY = 2
+MEET = 5
 VMEM_LIMIT = 60 * 1024 * 1024
 MESH = pl.DeviceIdType.MESH
 BF16 = jnp.bfloat16
@@ -131,9 +132,14 @@
     extra = sum(jnp.where(one, 1, 0) for one in crossing)
     pl.semaphore_wait(barrier, chips + 2 + jnp.where(inner, 1, 0) + extra)
 
+    share = pl.ds(pl.multiple_of(core * (domain // 2), domain // 2), domain // 2)
     pair_copy = pltpu.make_async_remote_copy(
-        potential_in.at[0], potential.at[odd], pair_sem.at[0], pair_sem.at[1],
-        {"clique": partner}, MESH,
+        potential_in.at[0, share], potential.at[odd, share],
+        pair_sem.at[0], pair_sem.at[1], {"clique": partner}, MESH,
+    )
+    relay = pltpu.make_async_remote_copy(
+        potential.at[1 - odd, share], potential.at[1 - odd, share],
+        pair_sem.at[2], pair_sem.at[3], {"dp": twin}, MESH,
     )
     pair_copy.start()
     f_copy = pltpu.make_async_remote_copy(
@@ -185,12 +191,18 @@
             g_copy.start()
             g_cross.start()
 
+    def pass_on():
+        pair_copy.wait_recv()
+        relay.start()
+
+    def take_partner():
+        relay.wait_recv()
+        prepare(1 - odd)
+
     def pair_product():
-        pair_copy.wait_recv()
-        prepare(1 - odd)
-
         @pl.when(inner)
         def _():
+            take_partner()
             product = jnp.dot(q_high[0], q_high[1], preferred_element_type=F32)
             product += jnp.dot(q_high[0], q_low[1], preferred_element_type=F32)
             product += jnp.dot(q_low[0], q_high[1], preferred_element_type=F32)
@@ -238,6 +250,7 @@
 
             done = quarter * pairs + pair
             pl.when(done == 1)(second_messages)
+            pl.when(done == min(RELAY, meet))(pass_on)
 
             @pl.when(done == meet)
             def _():
@@ -272,6 +285,7 @@
             copy.start()
             second_trip.append(copy)
 
+    pl.when(jnp.logical_not(inner))(take_partner)
     stage(groups - 1)
 
     f_own[...] = f_in[...]
@@ -329,6 +343,7 @@
         copy.wait_send()
 
     pair_copy.wait_send()
+    relay.wait_send()
     for copy in [put_beliefs] + halves:
         copy.wait()
 
@@ -407,7 +422,7 @@
             dma((QUARTERS,)),
             dma((2,)),
             dma((3,)),
-            dma((2,)),
+            dma((4,)),
             dma((3,)),
             dma((3,)),
             dma((PIECES,)),

time: 26.7 us -> 23.9 us (0.90)
  Pallas kernels: 25.9 us -> 23.1 us
    pallas_call x1, Pallas kernels: 24.1 us -> 21.3 us  [per_device(): pl.pallas_call(functools.partial(kernel, (cliques, copies), scale), out_s...]
where the time goes in v2:
time: 23.9 us; the launch traced here: 23.7 us
  Pallas kernels  23.1 us (97%)
  between operations  0.64 us (3%)
    pallas_call x1, Pallas kernels, per_device(): pl.pallas_call(functools.partial(kernel, (cliques, copies), scale), out_s...  21.3 us
    pallas_call x1, Pallas kernels, per_device(): pl.pallas_call(hand_on, out_shape=(table, table), in_specs=[hbm, hbm], ou...  1.82 us

profile of v2, /device:TPU:1, one launch (start us, length us, event | category | flops | bytes accessed | tf_op | source)
XLA Modules:
  0.0 23.7 jit_solution(4071465949491725875)
XLA Ops:
  0.6 21.3 %shard_map.59 = (f32[256,256]{1,0:T(8,128)}, f32[256,256]{1,0:T(8,128)}) custom-call(s32[9]{0:T(128)} %order.1, s32[9,65536]{1,0:T(8,128)} %table.1, f32[1,256,256]{2,1,0:T(8,128)} %potential_in.1, f32[1,256,256]{2,1,0:T(8,128)} %noise_in.1), custom_call_target="tpu_custom_call" | custom-call | tf_op jit(solution)/shard_map/pallas_call | solution.py:394
  21.9 1.8 %shard_map.60 = (f32[256,256]{1,0:T(8,128)}, f32[256,256]{1,0:T(8,128)}) custom-call(f32[256,256]{1,0:T(8,128)} %get-tuple-element.6.updated, f32[256,256]{1,0:T(8,128)} %get-tuple-element.7.beliefs), custom_call_target="tpu_custom_call" | custom-call | tf_op jit(solution)/shard_map/pallas_call | solution.py:439
